TPU v7x, 128 devices: a whole 4x4x4 slice. The times are simulated.
128 devices in a mesh: gy: 8 (over x, core), gz: 16 (over y, z).
Axes of the slice: x: 4, y: 4, z: 4, core: 2. Of those that a mesh axis runs over, the one named last changes fastest.
Arguments:
- velocity: float32 [3, 768, 12288], P(None, 'gy', 'gz'), may hold values from -250 to 250
- strain: bfloat16 [6, 768, 12288], P(None, 'gy', 'gz'), may hold values from -250 to 250
- cell_height: float32 [768], P('gy'), may hold values from 0.5 to 2
- stencil_reach: int32 [2, 768], P(None, 'gy'), may hold values from 1 to 8, as said below
Outputs:
- coefficient: float32 [768], P('gy')
Inputs may be any that keep to these rules, and one draw needn't show every extreme that they name: `stencil_reach`: in every draw some plane reaches 8 planes on both sides; stencils are cut at the walls by the steps.
All inputs are finite; a program needn't handle non-finite values.
Results may differ from a plain program's by a relative error of at most 0.0003.
Values sent between devices are 32-bit elements; how exact they have to be, the bound alone decides.
No kernel may reach another device: no remote copies, remote signals or barrier semaphores. Data moves between devices by JAX's collectives and lax.ppermute only.
A program may use at most 128 MiB of HBM per device.

v0:
```python
import jax
import jax.numpy as jnp
from jax import lax
from jax.sharding import PartitionSpec as P

NX = 8
HMAX = 8
LEAD_INDEX = (0, 1, 2, 0, 0, 1)
TAIL_INDEX = (0, 1, 2, 1, 2, 2)
TENSOR_WEIGHTS = (1.0, 1.0, 1.0, 2.0, 2.0, 2.0)


def extended(cells, sides, width, closed):
    for axis, dim in sides:
        count = lax.axis_size(axis)
        ends = count if closed else count - 1
        head = lax.slice_in_dim(cells, 0, width, axis=dim)
        tail = lax.slice_in_dim(cells, cells.shape[dim] - width, cells.shape[dim], axis=dim)
        cells = jnp.concatenate(
            [
                lax.ppermute(tail, axis, [(i, (i + 1) % count) for i in range(ends)]),
                cells,
                lax.ppermute(head, axis, [((i + 1) % count, i) for i in range(ends)]),
            ],
            axis=dim,
        )
    return cells


def strain_rate(tensor):
    squares = 2.0 * (tensor[0] * tensor[0] + tensor[1] * tensor[1] + tensor[2] * tensor[2])
    squares = squares + 4.0 * (
        tensor[3] * tensor[3] + tensor[4] * tensor[4] + tensor[5] * tensor[5]
    )
    return jnp.sqrt(squares)


def form_fields(velocity, tensor):
    products = jnp.stack(
        [
            velocity[first_index] * velocity[second_index]
            for first_index, second_index in zip(LEAD_INDEX, TAIL_INDEX)
        ]
    )
    magnitude = strain_rate(tensor)
    return jnp.concatenate([velocity, products, tensor, magnitude[None] * tensor], axis=0)


def streamwise_filter(fields):
    length = fields.shape[-1]
    position = jnp.arange(length, dtype=jnp.int32) % NX
    behind = jnp.where(
        position == 0, jnp.roll(fields, 1 - NX, axis=-1), jnp.roll(fields, 1, axis=-1)
    )
    ahead_cells = jnp.where(
        position == NX - 1, jnp.roll(fields, NX - 1, axis=-1), jnp.roll(fields, -1, axis=-1)
    )
    return 0.25 * behind + 0.5 * fields + 0.25 * ahead_cells


def spanwise_filter(widened):
    return (
        0.25 * widened[..., : -2 * NX] + 0.5 * widened[..., NX:-NX] + 0.25 * widened[..., 2 * NX :]
    )


def band_apply(band_matrix, padded):
    flattened = padded.reshape(padded.shape[0], padded.shape[1], -1)
    result = jnp.einsum("jc,fcm->fjm", band_matrix, flattened, precision=lax.Precision.HIGHEST)
    return result.reshape((padded.shape[0], band_matrix.shape[0]) + padded.shape[2:])


def contraction(filtered, sum_axes):
    velocity_bar = filtered[0:3]
    product_bar = filtered[3:9]
    tensor_bar = filtered[9:15]
    model_bar = filtered[15:21]
    rate_bar = strain_rate(tensor_bar)
    numerator = jnp.zeros(filtered.shape[1:], jnp.float32)
    denominator = jnp.zeros(filtered.shape[1:], jnp.float32)
    for component in range(6):
        leonard = (
            product_bar[component]
            - velocity_bar[LEAD_INDEX[component]] * velocity_bar[TAIL_INDEX[component]]
        )
        model_term = model_bar[component] - 4.0 * rate_bar * tensor_bar[component]
        numerator = numerator + TENSOR_WEIGHTS[component] * leonard * model_term
        denominator = denominator + TENSOR_WEIGHTS[component] * model_term * model_term
    return (jnp.sum(numerator, axis=sum_axes), jnp.sum(denominator, axis=sum_axes))


def local(velocity, strain, cell_height, stencil_reach):
    planes = velocity.shape[1]
    cell_count = velocity.shape[2]
    total_planes = lax.axis_size("gy") * planes
    total_cells = lax.axis_size("gz") * cell_count
    heights = extended(cell_height, (("gy", 0),), HMAX, False)
    offset = lax.axis_index("gy") * planes
    rows_global = offset + jnp.arange(planes, dtype=jnp.int32)
    columns_global = offset - HMAX + jnp.arange(planes + 2 * HMAX, dtype=jnp.int32)
    lowest = jnp.maximum(rows_global - stencil_reach[0], 0)
    highest = jnp.minimum(rows_global + stencil_reach[1], total_planes - 1)
    inside = (columns_global[None, :] >= lowest[:, None]) & (
        columns_global[None, :] <= highest[:, None]
    )
    weights = jnp.where(inside, heights[None, :], 0.0)
    band_matrix = weights / jnp.sum(weights, axis=1, keepdims=True)
    raw_inputs = jnp.concatenate([velocity, strain.astype(jnp.float32)], axis=0)
    fields = form_fields(raw_inputs[0:3], raw_inputs[3:9])
    widened = extended(streamwise_filter(fields), (("gz", 2),), NX, True)
    spanwise = spanwise_filter(widened)
    full_band = lax.all_gather(band_matrix, "gy", axis=0, tiled=True)
    block_count = lax.axis_size("gy")
    grouped = spanwise.reshape(spanwise.shape[0], planes, block_count, cell_count // block_count)
    padded = jnp.pad(
        lax.all_to_all(grouped, "gy", split_axis=2, concat_axis=1, tiled=True),
        ((0, 0), (HMAX, HMAX), (0, 0), (0, 0)),
    )
    sections = [
        band_apply(
            full_band[block_index * planes : (block_index + 1) * planes],
            padded[:, block_index * planes : block_index * planes + planes + 2 * HMAX],
        )
        for block_index in range(block_count)
    ]
    filtered = jnp.concatenate(sections, axis=1)
    numerator, denominator = contraction(filtered, 1)
    numerator = jnp.sum(numerator, axis=1)
    denominator = jnp.sum(denominator, axis=1)
    numerator, denominator = lax.psum((numerator, denominator), ("gy", "gz"))
    whole = numerator / total_cells / (denominator / total_cells + 1e-06)
    return lax.dynamic_slice_in_dim(whole, offset, planes)


def solution(mesh):
    in_specs = (P(None, "gy", "gz"), P(None, "gy", "gz"), P("gy"), P(None, "gy"))
    out_specs = P("gy")
    return jax.shard_map(local, mesh=mesh, in_specs=in_specs, out_specs=out_specs, check_vma=False)
```

profile of v0, /device:TPU:1, one launch (start us, length us, event | category | flops | bytes accessed | tf_op | source)
XLA Modules:
  0.0 296.6 jit_solution(2417976112965533351)
XLA Ops:
  0.0 0.0 copy-start.1
  0.0 1.6 copy.30
  1.6 1.2 constant_dynamic-update-slice_fusion
  2.8 0.8 multiply_dynamic-update-slice_fusion.6
  3.6 0.8 multiply_dynamic-update-slice_fusion.5
  4.4 0.8 multiply_dynamic-update-slice_fusion.4
  5.1 0.8 multiply_dynamic-update-slice_fusion.3
  6.0 0.8 multiply_dynamic-update-slice_fusion.2
  6.8 0.8 multiply_dynamic-update-slice_fusion.1
  7.5 0.0 copy-done.1
  7.6 0.7 copy.29
  8.3 0.2 convert_element_type.5
  8.4 1.7 convert_dynamic-update-slice_fusion
  10.1 0.3 fusion.16
  10.4 1.6 multiply_dynamic-update-slice_fusion
  12.0 9.7 %fusion.62 = (f32[21,96,767]{1,2,0:T(8,128)S(1)}, f32[21,96,767]{1,2,0:T(8,128)}) fusion(f32[21,96,768]{1,2,0:T(8,128)} %multiply_dynamic-update-slice_fusion), kind=kLoop, calls=%fused_computation.136 | loop fusion | bytes 24740352 | tf_op jit(solution)/shard_map/jit(_roll_static)/slice | solution.py:56
  21.7 10.9 %fusion.65 = (f32[21,96,761]{1,2,0:T(8,128)}, f32[21,96,761]{1,2,0:T(8,128)}) fusion(f32[21,96,768]{1,2,0:T(8,128)} %multiply_dynamic-update-slice_fusion), kind=kLoop, calls=%fused_computation.139 | loop fusion | bytes 24546816 | tf_op jit(solution)/shard_map/jit(_roll_static)/slice | solution.py:56
  32.6 0.9 fusion.64
  33.5 0.9 fusion.63
  34.5 15.5 %fusion.6 = f32[21,96,768]{1,2,0:T(8,128)S(1)} fusion(f32[21,96,7]{1,2,0:T(8,128)S(1)} %get-tuple-element.16, f32[21,96,761]{1,2,0:T(8,128)} %get-tuple-element.18, f32[21,96,767]{1,2,0:T(8,128)} %get-tuple-element.12, f32[21,96,1]{1,2,0:T(1,128)S(1)} %get-tuple-element.14, f32[21,96,761]{1,2,0:T(8,128)} %get-tuple-element.17, ...), kind=kLoop, calls=%fused_computation.9 | loop fusion | flops 17031168 | bytes 37160448 | tf_op jit(solution)/shard_map/add | solution.py:58
  50.0 2.5 collective-permute-start
  52.5 4.7 %collective-permute-start.1 = (f32[21,96,8]{1,2,0:T(8,128)S(1)}, f32[21,96,8]{1,2,0:T(8,128)S(1)}, u32[]{:S(2)}, u32[]{:S(2)}) collective-permute-start(f32[21,96,8]{1,2,0:T(8,128)S(1)} %get-tuple-element.10), channel_id=1, source_target_pairs={{1,0},{2,1},{3,2},{4,3},{5,4},{6,5},{7,6},{8,7},{9,8},{10,9},{11,1... | collective-permute-start | bytes 193544 | tf_op jit(solution)/shard_map/ppermute | solution.py:23
  57.2 2.2 collective-permute-done
  59.4 0.0 collective-permute-done.1
  59.4 2.4 fusion.1
  61.8 3.9 %copy.31 = f32[21,96,8,96]{1,3,0,2:T(8,128)} copy(f32[21,96,8,96]{1,3,2,0:T(8,128)S(1)} %bitcast.280) | data formatting | bytes 12386304 | tf_op jit(solution)/shard_map/reshape | solution.py:114
  65.7 0.0 copy-start.2
  65.7 0.0 copy-start.3
  65.7 6.2 %all-to-all-start = ((f32[21,96,8,96]{1,3,0,2:T(8,128)}), f32[21,96,8,96]{1,3,0,2:T(8,128)}, u32[]{:S(2)}, u32[]{:S(2)}) async-start(f32[21,96,8,96]{1,3,0,2:T(8,128)} %copy.31), calls=%async_computation | async-start | bytes 16515072 | tf_op jit(solution)/shard_map/all_to_all | solution.py:116
  71.9 0.0 copy-done.2
  71.9 0.1 fusion.66
  72.0 3.5 %collective-permute-start.2 = (f32[8]{0:T(128)S(1)}, f32[8]{0:T(128)S(1)}, u32[]{:S(2)}, u32[]{:S(2)}) collective-permute-start(f32[8]{0:T(128)S(1)} %get-tuple-element.21), channel_id=1, source_target_pairs={{0,16},{16,32},{32,48},{48,64},{64,80},{80,96},{96,112},{1,17},{17... | collective-permute-start | bytes 104 | tf_op jit(solution)/shard_map/ppermute | solution.py:21
  75.5 1.9 collective-permute-start.3
  77.5 0.0 copy-done.3
  77.5 83.5 %collective-permute-done.2 = f32[8]{0:T(128)S(1)} collective-permute-done((f32[8]{0:T(128)S(1)}, f32[8]{0:T(128)S(1)}, u32[]{:S(2)}, u32[]{:S(2)}) %collective-permute-start.2) | collective-permute-done | bytes 64 | tf_op jit(solution)/shard_map/ppermute | solution.py:21
  160.9 2.4 collective-permute-done.3
  163.3 0.1 pad_maximum_fusion.2
  163.4 0.2 select_reduce_fusion
  163.6 0.1 select_divide_fusion
  163.7 11.9 %all_gather.3 = f32[768,112]{1,0:T(8,128)S(1)} all-gather(f32[96,112]{1,0:T(8,128)S(1)} %select_divide_fusion), channel_id=1, replica_groups=mesh['gy'=8,'gz'=16] {'gy'}, dimensions={0}, use_global_device_ids=true | all-gather | bytes 387072 | tf_op jit(solution)/shard_map/all_gather | solution.py:112
  175.6 0.0 all-to-all-done
  175.6 13.4 %copy.32 = f32[21,8,96,1,96]{2,1,4,0,3:T(8,128)} copy(f32[21,8,96,1,96]{2,4,0,1,3:T(8,128)} %bitcast.3) | data formatting | bytes 12386304 | tf_op jit(solution)/shard_map/all_to_all | solution.py:116
  189.0 9.5 %all_to_all.16 = f32[21,768,1,96]{1,3,0,2:T(8,128)} reshape(f32[21,8,96,1,96]{2,1,4,0,3:T(8,128)} %copy.32) | data formatting | bytes 12386304 | tf_op jit(solution)/shard_map/all_to_all | solution.py:116
  198.5 0.0 copy-start
  198.5 2.4 convolution_bitcast_fusion
  200.9 2.6 convolution_bitcast_fusion.1
  203.5 0.0 copy-done
  203.5 2.0 convolution_bitcast_fusion.2
  205.5 2.0 convolution_bitcast_fusion.3
  207.5 2.1 convolution_bitcast_fusion.4
  209.5 2.0 convolution_bitcast_fusion.5
  211.5 2.0 convolution_bitcast_fusion.6
  213.5 1.0 convolution_bitcast_fusion.7
  214.6 8.9 %concatenate.40 = f32[21,768,1,96]{1,3,0,2:T(8,128)} concatenate(f32[21,96,1,96]{1,3,0,2:T(8,128)S(1)} %convolution_bitcast_fusion.7, f32[21,96,1,96]{1,3,0,2:T(8,128)} %convolution_bitcast_fusion.6, f32[21,96,1,96]{1,3,0,2:T(8,128)} %convolution_bitcast_fusion.5, f32[21,96,1,96]{1,3,0,2:T(8,128)} %convolution_bitcast_fusion.4, f32[21,96,1,96]{1,3,0,2:T(8,128)} %convolution_bitcast_fusion.3, ...), dimensions={1} | concatenate | bytes 12386304 | tf_op jit(solution)/shard_map/concatenate | solution.py:126
  223.4 3.3 %fusion.30 = (f32[768]{0:T(1024)S(1)}, f32[768,96]{0,1:T(8,128)S(1)}) fusion(f32[21,768,1,96]{1,3,2,0:T(8,128)} %bitcast.278, f32[21,768,1,96]{1,3,0,2:T(8,128)} %concatenate.40), kind=kLoop, calls=%fused_computation.67 | loop fusion | flops 3906816 | bytes 6491136 | tf_op jit(solution)/shard_map/reduce_sum | solution.py:128
  226.7 2.2 fusion.24
  229.0 67.1 %all-reduce.1 = (f32[768]{0:T(1024)S(1)}, f32[768]{0:T(1024)S(1)}) all-reduce(f32[768]{0:T(1024)S(1)} %fusion.24, f32[768]{0:T(1024)S(1)} %get-tuple-element.7), channel_id=1, replica_groups=mesh['gy'=8,'gz'=16] {'gy','gz'}, use_global_device_ids=true, to_apply=%region_4.5 | all-reduce | flops 1536 | bytes 12288 | tf_op jit(solution)/shard_map/psum | solution.py:130
  296.0 0.6 dynamic_slice.3
  (5 shorter events, 0.0 us)
Async XLA Ops:
  0.0 7.5 %copy-start.1 = (bf16[6,96,768]{2,1,0:T(8,128)(2,1)S(1)}, bf16[6,96,768]{2,1,0:T(8,128)(2,1)}, u32[]{:S(2)}) copy-start(bf16[6,96,768]{2,1,0:T(8,128)(2,1)} %param.5) | copy-start | bytes 2654212
  50.0 9.4 %collective-permute-start = (f32[21,96,8]{1,2,0:T(8,128)S(1)}, f32[21,96,8]{1,2,0:T(8,128)S(1)}, u32[]{:S(2)}, u32[]{:S(2)}) collective-permute-start(f32[21,96,8]{1,2,0:T(8,128)S(1)} %get-tuple-element.9), channel_id=1, source_target_pairs={{0,1},{1,2},{2,3},{3,4},{4,5},{5,6},{6,7},{7,8},{8,9},{9,10},{10,1... | collective-permute-start | bytes 193544 | tf_op jit(solution)/shard_map/ppermute | solution.py:21
  52.5 6.8 %collective-permute-start.1 = (f32[21,96,8]{1,2,0:T(8,128)S(1)}, f32[21,96,8]{1,2,0:T(8,128)S(1)}, u32[]{:S(2)}, u32[]{:S(2)}) collective-permute-start(f32[21,96,8]{1,2,0:T(8,128)S(1)} %get-tuple-element.10), channel_id=1, source_target_pairs={{1,0},{2,1},{3,2},{4,3},{5,4},{6,5},{7,6},{8,7},{9,8},{10,9},{11,1... | collective-permute-start | bytes 193544 | tf_op jit(solution)/shard_map/ppermute | solution.py:23
  65.7 6.2 %copy-start.2 = (f32[96]{0:T(128)S(1)}, f32[96]{0:T(128)}, u32[]{:S(2)}) copy-start(f32[96]{0:T(128)} %param.6) | copy-start | bytes 1156
  65.7 11.7 %copy-start.3 = (s32[2,96]{1,0:T(2,128)S(1)}, s32[2,96]{1,0:T(2,128)}, u32[]{:S(2)}) copy-start(s32[2,96]{1,0:T(2,128)} %param.7) | copy-start | bytes 2308
  65.7 109.9 %all-to-all-start = ((f32[21,96,8,96]{1,3,0,2:T(8,128)}), f32[21,96,8,96]{1,3,0,2:T(8,128)}, u32[]{:S(2)}, u32[]{:S(2)}) async-start(f32[21,96,8,96]{1,3,0,2:T(8,128)} %copy.31), calls=%async_computation | async-start | bytes 16515072 | tf_op jit(solution)/shard_map/all_to_all | solution.py:116
  72.0 89.0 %collective-permute-start.2 = (f32[8]{0:T(128)S(1)}, f32[8]{0:T(128)S(1)}, u32[]{:S(2)}, u32[]{:S(2)}) collective-permute-start(f32[8]{0:T(128)S(1)} %get-tuple-element.21), channel_id=1, source_target_pairs={{0,16},{16,32},{32,48},{48,64},{64,80},{80,96},{96,112},{1,17},{17... | collective-permute-start | bytes 104 | tf_op jit(solution)/shard_map/ppermute | solution.py:21
  75.5 87.8 %collective-permute-start.3 = (f32[8]{0:T(128)S(1)}, f32[8]{0:T(128)S(1)}, u32[]{:S(2)}, u32[]{:S(2)}) collective-permute-start(f32[8]{0:T(128)S(1)} %get-tuple-element.22), channel_id=1, source_target_pairs={{16,0},{32,16},{48,32},{64,48},{80,64},{96,80},{112,96},{17,1},{33... | collective-permute-start | bytes 104 | tf_op jit(solution)/shard_map/ppermute | solution.py:23
  198.5 5.0 %copy-start = (f32[21,768,1,96]{1,3,0,2:T(8,128)S(1)}, f32[21,768,1,96]{1,3,0,2:T(8,128)}, u32[]{:S(2)}) copy-start(f32[21,768,1,96]{1,3,0,2:T(8,128)} %all_to_all.16) | copy-start | bytes 18579460
where the time goes:
time: 297 us
  waiting for transfers between devices  88 us (30%)
  blocking collectives  79 us (27%)
  local copies, waits for them, and re-layouts  62.3 us (21%)
  other arithmetic  32.3 us (11%)
  starting transfers between devices  18.8 us (6%)
  matrix products  16 us (5%)
    ppermute x2, waiting for transfers between devices, extended(): lax.ppermute(tail, axis, [(i, (i + 1) % count) for i in range(ends)])  85.6 us
    psum x1, blocking collectives, local(): numerator, denominator = lax.psum((numerator, denominator), ('gy', 'gz'))  67.1 us
    all_to_all x2, local copies, waits for them, and re-layouts, local(): lax.all_to_all(grouped, 'gy', split_axis=2, concat_axis=1, tiled=True)  22.9 us
    dot_general x8, matrix products, band_apply(): jnp.einsum('jc,fcm->fjm', band_matrix, flattened, precision=lax.Precision...  16 us
    add x1, other arithmetic, streamwise_filter(): return 0.25 * behind + 0.5 * fields + 0.25 * ahead_cells  15.5 us
    all_gather x1, blocking collectives, local(): full_band = lax.all_gather(band_matrix, 'gy', axis=0, tiled=True)  11.9 us
    slice x2, local copies, waits for them, and re-layouts, streamwise_filter(): jnp.roll(fields, NX - 1, axis=-1)  11.9 us
    slice x2, local copies, waits for them, and re-layouts, streamwise_filter(): jnp.roll(fields, -1, axis=-1)  10.6 us
  transfers between devices with their start and end apart: 5, of which 3 were waited for; matrix products, arithmetic and copies ran while one was open for 0% of the time, Pallas kernels for 0%

commit v1 on v0

--- a/solution.py
+++ b/solution.py
@@ -127,7 +127,8 @@
     numerator, denominator = contraction(filtered, 1)
     numerator = jnp.sum(numerator, axis=1)
     denominator = jnp.sum(denominator, axis=1)
-    numerator, denominator = lax.psum((numerator, denominator), ("gy", "gz"))
+    take_panel = lambda x_in: lax.psum(lax.psum(x_in, "gy"), axis_name="gz")
+    numerator, denominator = take_panel((numerator, denominator))
     whole = numerator / total_cells / (denominator / total_cells + 1e-06)
     return lax.dynamic_slice_in_dim(whole, offset, planes)
 

time: 297 us -> 286 us (0.963)
  the two profiles are of different devices: /device:TPU:1 before, /device:TPU:0 now
where the time goes in v1:
time: 286 us; the launch traced here: 285 us
  blocking collectives  154 us (54%)
  local copies, waits for them, and re-layouts  62.3 us (22%)
  other arithmetic  32.3 us (11%)
  matrix products  16 us (6%)
  starting transfers between devices  15.3 us (5%)
  waiting for transfers between devices  5.26 us (2%)
    all_gather x1, blocking collectives, local(): full_band = lax.all_gather(band_matrix, 'gy', axis=0, tiled=True)  96.8 us
    psum x2, blocking collectives, local(): take_panel = lambda x_in: lax.psum(lax.psum(x_in, 'gy'), axis_name='gz')  56.9 us
    all_to_all x2, local copies, waits for them, and re-layouts, local(): lax.all_to_all(grouped, 'gy', split_axis=2, concat_axis=1, tiled=True)  22.9 us
    dot_general x8, matrix products, band_apply(): jnp.einsum('jc,fcm->fjm', band_matrix, flattened, precision=lax.Precision...  16 us
    add x1, other arithmetic, streamwise_filter(): return 0.25 * behind + 0.5 * fields + 0.25 * ahead_cells  15.5 us
    slice x2, local copies, waits for them, and re-layouts, streamwise_filter(): jnp.roll(fields, NX - 1, axis=-1)  11.8 us
    slice x2, local copies, waits for them, and re-layouts, streamwise_filter(): jnp.roll(fields, -1, axis=-1)  10.6 us
    concatenate x1, local copies, waits for them, and re-layouts, local(): filtered = jnp.concatenate(sections, axis=1)  8.87 us
  transfers between devices with their start and end apart: 5, of which 2 were waited for; matrix products, arithmetic and copies ran while one was open for 0% of the time, Pallas kernels for 0%

profile of v1, /device:TPU:0, one launch (start us, length us, event | category | flops | bytes accessed | tf_op | source)
XLA Modules:
  0.0 285.1 jit_solution(5808550794841654113)
XLA Ops:
  0.0 0.0 copy-start.1
  0.0 1.6 copy.30
  1.6 1.2 constant_dynamic-update-slice_fusion
  2.8 0.8 multiply_dynamic-update-slice_fusion.6
  3.6 0.8 multiply_dynamic-update-slice_fusion.5
  4.4 0.8 multiply_dynamic-update-slice_fusion.4
  5.1 0.8 multiply_dynamic-update-slice_fusion.3
  6.0 0.8 multiply_dynamic-update-slice_fusion.2
  6.8 0.8 multiply_dynamic-update-slice_fusion.1
  7.6 0.0 copy-done.1
  7.6 0.7 copy.29
  8.3 0.2 convert_element_type.5
  8.4 1.7 convert_dynamic-update-slice_fusion
  10.1 0.3 fusion.16
  10.4 1.6 multiply_dynamic-update-slice_fusion
  12.0 9.7 %fusion.62 = (f32[21,96,767]{1,2,0:T(8,128)S(1)}, f32[21,96,767]{1,2,0:T(8,128)}) fusion(f32[21,96,768]{1,2,0:T(8,128)} %multiply_dynamic-update-slice_fusion), kind=kLoop, calls=%fused_computation.136 | loop fusion | bytes 24740352 | tf_op jit(solution)/shard_map/jit(_roll_static)/slice | solution.py:56
  21.6 10.9 %fusion.65 = (f32[21,96,761]{1,2,0:T(8,128)}, f32[21,96,761]{1,2,0:T(8,128)}) fusion(f32[21,96,768]{1,2,0:T(8,128)} %multiply_dynamic-update-slice_fusion), kind=kLoop, calls=%fused_computation.139 | loop fusion | bytes 24546816 | tf_op jit(solution)/shard_map/jit(_roll_static)/slice | solution.py:56
  32.5 0.9 fusion.64
  33.5 0.9 fusion.63
  34.4 15.5 %fusion.6 = f32[21,96,768]{1,2,0:T(8,128)S(1)} fusion(f32[21,96,7]{1,2,0:T(8,128)S(1)} %get-tuple-element.18, f32[21,96,761]{1,2,0:T(8,128)} %get-tuple-element.20, f32[21,96,767]{1,2,0:T(8,128)} %get-tuple-element.14, f32[21,96,1]{1,2,0:T(1,128)S(1)} %get-tuple-element.16, f32[21,96,761]{1,2,0:T(8,128)} %get-tuple-element.19, ...), kind=kLoop, calls=%fused_computation.9 | loop fusion | flops 17031168 | bytes 37160448 | tf_op jit(solution)/shard_map/add | solution.py:58
  49.9 2.1 collective-permute-start
  52.0 4.7 %collective-permute-start.1 = (f32[21,96,8]{1,2,0:T(8,128)S(1)}, f32[21,96,8]{1,2,0:T(8,128)S(1)}, u32[]{:S(2)}, u32[]{:S(2)}) collective-permute-start(f32[21,96,8]{1,2,0:T(8,128)S(1)} %get-tuple-element.12), channel_id=1, source_target_pairs={{1,0},{2,1},{3,2},{4,3},{5,4},{6,5},{7,6},{8,7},{9,8},{10,9},{11,1... | collective-permute-start | bytes 193544 | tf_op jit(solution)/shard_map/ppermute | solution.py:23
  56.6 2.4 collective-permute-done
  59.1 0.0 collective-permute-done.1
  59.1 2.4 fusion.1
  61.5 3.9 %copy.31 = f32[21,96,8,96]{1,3,0,2:T(8,128)} copy(f32[21,96,8,96]{1,3,2,0:T(8,128)S(1)} %bitcast.280) | data formatting | bytes 12386304 | tf_op jit(solution)/shard_map/reshape | solution.py:114
  65.5 0.0 copy-start.2
  65.5 0.0 copy-start.3
  65.5 5.1 %all-to-all-start = ((f32[21,96,8,96]{1,3,0,2:T(8,128)}), f32[21,96,8,96]{1,3,0,2:T(8,128)}, u32[]{:S(2)}, u32[]{:S(2)}) async-start(f32[21,96,8,96]{1,3,0,2:T(8,128)} %copy.31), calls=%async_computation | async-start | bytes 16515072 | tf_op jit(solution)/shard_map/all_to_all | solution.py:116
  70.5 0.0 copy-done.2
  70.5 0.1 fusion.66
  70.6 2.3 collective-permute-start.2
  72.9 1.3 collective-permute-start.3
  74.2 0.0 copy-done.3
  74.2 0.0 collective-permute-done.2
  74.2 2.8 collective-permute-done.3
  77.0 0.1 pad_maximum_fusion.2
  77.1 0.2 select_reduce_fusion
  77.3 0.1 select_divide_fusion
  77.4 96.8 %all_gather.3 = f32[768,112]{1,0:T(8,128)S(1)} all-gather(f32[96,112]{1,0:T(8,128)S(1)} %select_divide_fusion), channel_id=1, replica_groups=mesh['gy'=8,'gz'=16] {'gy'}, dimensions={0}, use_global_device_ids=true | all-gather | bytes 387072 | tf_op jit(solution)/shard_map/all_gather | solution.py:112
  174.3 0.0 all-to-all-done
  174.3 13.4 %copy.32 = f32[21,8,96,1,96]{2,1,4,0,3:T(8,128)} copy(f32[21,8,96,1,96]{2,4,0,1,3:T(8,128)} %bitcast.3) | data formatting | bytes 12386304 | tf_op jit(solution)/shard_map/all_to_all | solution.py:116
  187.7 9.5 %all_to_all.16 = f32[21,768,1,96]{1,3,0,2:T(8,128)} reshape(f32[21,8,96,1,96]{2,1,4,0,3:T(8,128)} %copy.32) | data formatting | bytes 12386304 | tf_op jit(solution)/shard_map/all_to_all | solution.py:116
  197.2 0.0 copy-start
  197.2 2.4 convolution_bitcast_fusion
  199.6 2.6 convolution_bitcast_fusion.1
  202.2 0.0 copy-done
  202.2 2.0 convolution_bitcast_fusion.2
  204.2 2.0 convolution_bitcast_fusion.3
  206.1 2.1 convolution_bitcast_fusion.4
  208.2 2.0 convolution_bitcast_fusion.5
  210.2 2.0 convolution_bitcast_fusion.6
  212.2 1.0 convolution_bitcast_fusion.7
  213.2 8.9 %concatenate.40 = f32[21,768,1,96]{1,3,0,2:T(8,128)} concatenate(f32[21,96,1,96]{1,3,0,2:T(8,128)S(1)} %convolution_bitcast_fusion.7, f32[21,96,1,96]{1,3,0,2:T(8,128)} %convolution_bitcast_fusion.6, f32[21,96,1,96]{1,3,0,2:T(8,128)} %convolution_bitcast_fusion.5, f32[21,96,1,96]{1,3,0,2:T(8,128)} %convolution_bitcast_fusion.4, f32[21,96,1,96]{1,3,0,2:T(8,128)} %convolution_bitcast_fusion.3, ...), dimensions={1} | concatenate | bytes 12386304 | tf_op jit(solution)/shard_map/concatenate | solution.py:126
  222.1 3.3 %fusion.30 = (f32[768]{0:T(1024)S(1)}, f32[768,96]{0,1:T(8,128)S(1)}) fusion(f32[21,768,1,96]{1,3,2,0:T(8,128)} %bitcast.278, f32[21,768,1,96]{1,3,0,2:T(8,128)} %concatenate.40), kind=kLoop, calls=%fused_computation.67 | loop fusion | flops 3906816 | bytes 6491136 | tf_op jit(solution)/shard_map/reduce_sum | solution.py:128
  225.4 2.2 fusion.24
  227.6 15.6 %all-reduce.2 = (f32[768]{0:T(1024)S(1)}, f32[768]{0:T(1024)S(1)}) all-reduce(f32[768]{0:T(1024)S(1)} %fusion.24, f32[768]{0:T(1024)S(1)} %get-tuple-element.9), channel_id=1, replica_groups=mesh['gy'=8,'gz'=16] {'gy'}, use_global_device_ids=true, to_apply=%region_5.6 | all-reduce | flops 1536 | bytes 12288 | tf_op jit(solution)/shard_map/psum | solution.py:130
  243.2 41.3 %all-reduce.1 = (f32[768]{0:T(1024)S(1)}, f32[768]{0:T(1024)S(1)}) all-reduce(f32[768]{0:T(1024)S(1)} %get-tuple-element.7, f32[768]{0:T(1024)S(1)} %get-tuple-element.8), channel_id=1, replica_groups=mesh['gy'=8,'gz'=16] {'gz'}, use_global_device_ids=true, to_apply=%region_6.7 | all-reduce | flops 1536 | bytes 12288 | tf_op jit(solution)/shard_map/psum | solution.py:130
  284.6 0.6 dynamic_slice.3
  (5 shorter events, 0.0 us)
Async XLA Ops:
  0.0 7.6 %copy-start.1 = (bf16[6,96,768]{2,1,0:T(8,128)(2,1)S(1)}, bf16[6,96,768]{2,1,0:T(8,128)(2,1)}, u32[]{:S(2)}) copy-start(bf16[6,96,768]{2,1,0:T(8,128)(2,1)} %param.5) | copy-start | bytes 2654212
  49.9 9.2 %collective-permute-start = (f32[21,96,8]{1,2,0:T(8,128)S(1)}, f32[21,96,8]{1,2,0:T(8,128)S(1)}, u32[]{:S(2)}, u32[]{:S(2)}) collective-permute-start(f32[21,96,8]{1,2,0:T(8,128)S(1)} %get-tuple-element.11), channel_id=1, source_target_pairs={{0,1},{1,2},{2,3},{3,4},{4,5},{5,6},{6,7},{7,8},{8,9},{9,10},{10,1... | collective-permute-start | bytes 193544 | tf_op jit(solution)/shard_map/ppermute | solution.py:21
  52.0 7.1 %collective-permute-start.1 = (f32[21,96,8]{1,2,0:T(8,128)S(1)}, f32[21,96,8]{1,2,0:T(8,128)S(1)}, u32[]{:S(2)}, u32[]{:S(2)}) collective-permute-start(f32[21,96,8]{1,2,0:T(8,128)S(1)} %get-tuple-element.12), channel_id=1, source_target_pairs={{1,0},{2,1},{3,2},{4,3},{5,4},{6,5},{7,6},{8,7},{9,8},{10,9},{11,1... | collective-permute-start | bytes 193544 | tf_op jit(solution)/shard_map/ppermute | solution.py:23
  65.5 5.1 %copy-start.2 = (f32[96]{0:T(128)S(1)}, f32[96]{0:T(128)}, u32[]{:S(2)}) copy-start(f32[96]{0:T(128)} %param.6) | copy-start | bytes 1156
  65.5 8.7 %copy-start.3 = (s32[2,96]{1,0:T(2,128)S(1)}, s32[2,96]{1,0:T(2,128)}, u32[]{:S(2)}) copy-start(s32[2,96]{1,0:T(2,128)} %param.7) | copy-start | bytes 2308
  65.5 108.8 %all-to-all-start = ((f32[21,96,8,96]{1,3,0,2:T(8,128)}), f32[21,96,8,96]{1,3,0,2:T(8,128)}, u32[]{:S(2)}, u32[]{:S(2)}) async-start(f32[21,96,8,96]{1,3,0,2:T(8,128)} %copy.31), calls=%async_computation | async-start | bytes 16515072 | tf_op jit(solution)/shard_map/all_to_all | solution.py:116
  70.6 3.6 %collective-permute-start.2 = (f32[8]{0:T(128)S(1)}, f32[8]{0:T(128)S(1)}, u32[]{:S(2)}, u32[]{:S(2)}) collective-permute-start(f32[8]{0:T(128)S(1)} %get-tuple-element.23), channel_id=1, source_target_pairs={{0,16},{16,32},{32,48},{48,64},{64,80},{80,96},{96,112},{1,17},{17... | collective-permute-start | bytes 104 | tf_op jit(solution)/shard_map/ppermute | solution.py:21
  72.9 4.2 %collective-permute-start.3 = (f32[8]{0:T(128)S(1)}, f32[8]{0:T(128)S(1)}, u32[]{:S(2)}, u32[]{:S(2)}) collective-permute-start(f32[8]{0:T(128)S(1)} %get-tuple-element.24), channel_id=1, source_target_pairs={{16,0},{32,16},{48,32},{64,48},{80,64},{96,80},{112,96},{17,1},{33... | collective-permute-start | bytes 104 | tf_op jit(solution)/shard_map/ppermute | solution.py:23
  197.2 5.0 %copy-start = (f32[21,768,1,96]{1,3,0,2:T(8,128)S(1)}, f32[21,768,1,96]{1,3,0,2:T(8,128)}, u32[]{:S(2)}) copy-start(f32[21,768,1,96]{1,3,0,2:T(8,128)} %all_to_all.16) | copy-start | bytes 18579460
